TPU v7x, 256 devices: a whole 4x4x8 slice. The times are simulated.
256 devices in a mesh: dp: 32 (over z, x_hi, core), tensor: 8 (over x_lo, y).
Axes of the slice: x: 4 (x_hi: 2, x_lo: 2; x = x_hi * 2 + x_lo), y: 4, z: 8, core: 2. Of those that a mesh axis runs over, the one named last changes fastest.
Arguments:
- tokens: bfloat16 [32768, 4096], P(('dp', 'tensor')), may hold values from -6 to 6
- norm_gain: float32 [4096], replicated, may hold values from 0.25 to 1.75
- norm_bias: float32 [4096], replicated, may hold values from -3 to 3
- qkv_weight: bfloat16 [4096, 6144], P('dp', 'tensor'), may hold values from -8 to 8
- out_weight: bfloat16 [2048, 4096], P('tensor', 'dp'), may hold values from -0.125 to 0.125
- match_weight: bfloat16 [4096, 512], P('dp'), may hold values from -0.09375 to 0.09375
- matcher_qkv: bfloat16 [512, 1536], replicated, may hold values from -12 to 12
- matcher_out: bfloat16 [512, 512], replicated, may hold values from -0.25 to 0.25
Outputs:
- features: bfloat16 [32768, 4096], P(('dp', 'tensor'))
- matched: bfloat16 [32768, 512], P(('dp', 'tensor'))
All inputs are finite; a program needn't handle non-finite values.
Results may differ from a plain program's by a relative error of at most 0.014.
Values may be sent and summed in bfloat16 or wider, within the bound.
No kernel may reach another device: no remote copies, remote signals or barrier semaphores. Data moves between devices by JAX's collectives and lax.ppermute only.
A program may use at most 128 MiB of HBM per device.

v0:
```python
import math

import jax
import jax.numpy as jnp
from jax import lax
from jax.sharding import PartitionSpec as P

HEAD_DIM = 128
MATCH_HEADS = 8


def shifted(block, axis, distance):
    devices = range(lax.axis_size(axis))
    route = [((i - distance) % len(devices), i) for i in devices]
    return lax.ppermute(block, axis, route)


def layer_norm(rows_in, norm_gain, norm_bias):
    values = rows_in.astype(jnp.float32)
    center = jnp.mean(values, axis=-1, keepdims=True)
    spread = jnp.mean((values - center) ** 2, axis=-1, keepdims=True)
    return ((values - center) * lax.rsqrt(spread + 1e-06) * norm_gain + norm_bias).astype(
        jnp.bfloat16
    )


def attend_tokens(queries, keys, values, score_scale):
    scores = (
        jnp.einsum("qhd,khd->hqk", queries, keys, preferred_element_type=jnp.float32) * score_scale
    )
    probs = jax.nn.softmax(scores, axis=-1).astype(jnp.bfloat16)
    mixed_output = jnp.einsum("hqk,khd->qhd", probs, values, preferred_element_type=jnp.float32)
    return mixed_output.astype(jnp.bfloat16)


def relay(sending):
    halfway = lax.axis_size("dp") // 2
    whole_image = lax.all_gather(sending, "tensor", axis=0, tiled=True)
    return shifted(whole_image, "dp", halfway)


def per_device(
    tokens, norm_gain, norm_bias, qkv_weight, out_weight, match_weight, matcher_qkv, matcher_out
):
    row_count = tokens.shape[0]
    width = matcher_out.shape[0]
    normed = layer_norm(tokens, norm_gain, norm_bias)
    all_normed = lax.all_gather(normed, "tensor", axis=0, tiled=True)
    patch_count = all_normed.shape[0]
    columns = all_normed
    projected = jnp.dot(
        columns,
        lax.all_gather(qkv_weight, "dp", axis=0, tiled=True),
        preferred_element_type=jnp.float32,
    ).astype(jnp.bfloat16)
    local_heads = qkv_weight.shape[1] // (3 * HEAD_DIM)
    projected = projected.reshape(patch_count, local_heads, 3, HEAD_DIM)
    attended = attend_tokens(
        projected[:, :, 0], projected[:, :, 1], projected[:, :, 2], 1.0 / math.sqrt(HEAD_DIM)
    )
    attended = attended.reshape(patch_count, local_heads * HEAD_DIM)
    head_terms = jnp.dot(
        attended,
        lax.all_gather(out_weight, "dp", axis=1, tiled=True),
        preferred_element_type=jnp.float32,
    )
    summed = lax.psum_scatter(head_terms, "tensor", scatter_dimension=0, tiled=True)
    features = (tokens.astype(jnp.float32) + summed).astype(jnp.bfloat16)
    columns = features
    descriptor = jnp.dot(
        columns,
        lax.all_gather(match_weight, "dp", axis=0, tiled=True),
        preferred_element_type=jnp.float32,
    ).astype(jnp.bfloat16)
    matcher_queries = jnp.dot(
        descriptor, matcher_qkv[:, :width], preferred_element_type=jnp.float32
    ).astype(jnp.bfloat16)
    partner_rows = relay(descriptor)
    key_values = jnp.dot(
        partner_rows, matcher_qkv[:, width:], preferred_element_type=jnp.float32
    ).astype(jnp.bfloat16)
    matcher_keys = key_values[:, :width]
    matcher_values = key_values[:, width:]
    key_count = key_values.shape[0]
    head_width = width // MATCH_HEADS
    mixed_output = attend_tokens(
        matcher_queries.reshape(row_count, MATCH_HEADS, head_width),
        matcher_keys.reshape(key_count, MATCH_HEADS, head_width),
        matcher_values.reshape(key_count, MATCH_HEADS, head_width),
        1.0 / math.sqrt(head_width),
    )
    mixed_output = mixed_output.reshape(row_count, width)
    matched = descriptor.astype(jnp.float32) + jnp.dot(
        mixed_output, matcher_out, preferred_element_type=jnp.float32
    )
    return (features, matched.astype(jnp.bfloat16))


def solution(mesh):
    return jax.shard_map(
        per_device,
        mesh=mesh,
        in_specs=(
            P(("dp", "tensor"), None),
            P(),
            P(),
            P("dp", "tensor"),
            P("tensor", "dp"),
            P("dp", None),
            P(),
            P(),
        ),
        out_specs=(P(("dp", "tensor"), None), P(("dp", "tensor"), None)),
        check_vma=False,
    )
```

profile of v0, /device:TPU:32, one launch (start us, length us, event | category | flops | bytes accessed | tf_op | source)
XLA Modules:
  0.0 656.4 jit_solution(6655120850066669053)
XLA Ops:
  7.2 0.0 copy-start
  7.2 0.0 all-gather.8.cloned.1.call-start
  7.2 0.7 all-gather.8.cloned.1.call-update
  7.9 0.0 all-gather.6.cloned.1.call-start
  8.0 1.5 convert_reduce_fusion
  9.4 1.7 fusion.12
  11.1 2.7 fusion.15
  13.8 0.0 all-gather.6.cloned.1.call-update
  13.8 0.0 all-gather.10.cloned.1.call-start
  13.9 0.7 all-gather.10.cloned.1.call-update
  14.5 0.0 reduce-scatter.2.cloned.1.call-start
  14.6 93.0 %all-gather.8.cloned.1.call-done = bf16[4096,768]{1,0:T(8,128)(2,1)} async-done(((bf16[128,768]{1,0:T(8,128)(2,1)}), bf16[4096,768]{1,0:T(8,128)(2,1)}) %all-gather.8.cloned.1.call-update) | async-done | bytes 6291472 | tf_op jit(solution)/shard_map/all_gather | solution.py:53
  107.6 93.9 %all-gather.6.cloned.1.call-done = bf16[1024,4096]{1,0:T(8,128)(2,1)} async-done(((bf16[128,4096]{1,0:T(8,128)(2,1)}), bf16[1024,4096]{1,0:T(8,128)(2,1)}) %all-gather.6.cloned.1.call-update) | async-done | bytes 8388624 | tf_op jit(solution)/shard_map/all_gather | solution.py:48
  201.5 11.0 %convolution_convert_fusion.1 = bf16[1024,768]{0,1:T(8,128)(2,1)S(1)} fusion(bf16[1024,4096]{1,0:T(8,128)(2,1)} %all-gather.6.cloned.1.call-done, bf16[4096,768]{1,0:T(8,128)(2,1)} %all-gather.8.cloned.1.call-done), kind=kOutput, calls=%fused_computation.25 | convolution fusion | flops 6443237376 | bytes 16252928 | tf_op jit(solution)/shard_map/dot_general | solution.py:51
  212.5 5.0 fusion.32
  217.5 4.1 fusion.19
  221.6 58.1 %all-gather.10.cloned.1.call-done = bf16[256,4096]{1,0:T(8,128)(2,1)} async-done(((bf16[256,128]{1,0:T(8,128)(2,1)}), bf16[256,4096]{1,0:T(8,128)(2,1)}) %all-gather.10.cloned.1.call-update) | async-done | bytes 2097168 | tf_op jit(solution)/shard_map/all_gather | solution.py:64
  279.7 9.7 %fusion.34 = f32[1024,4096]{1,0:T(8,128)} fusion(bf16[1024,256]{0,1:T(8,128)(2,1)S(1)} %bitcast.56, bf16[256,4096]{1,0:T(8,128)(2,1)} %all-gather.10.cloned.1.call-done), kind=kOutput, calls=%fused_computation.47 | convolution fusion | flops 2147483648 | bytes 19398656 | tf_op jit(solution)/shard_map/dot_general | solution.py:62
  289.4 0.0 copy-start.1
  289.4 0.0 reduce-scatter.2.cloned.1.call-update
  289.4 0.0 all-gather.12.cloned.1.call-start
  289.5 0.5 all-gather.12.cloned.1.call-update
  290.0 0.0 all-gather.14.cloned.1.call-start
  290.0 169.9 %reduce-scatter.2.cloned.1.call-done = f32[128,4096]{1,0:T(8,128)} async-done(((f32[1024,4096]{1,0:T(8,128)}), f32[128,4096]{1,0:T(8,128)}) %reduce-scatter.2.cloned.1.call-update) | async-done | bytes 2097168 | tf_op jit(solution)/shard_map/reduce_scatter | solution.py:67
  460.0 0.0 copy-done.1
  460.0 1.8 fusion.16
  461.8 0.0 copy-start.2
  461.8 85.9 %all-gather.12.cloned.1.call-done = bf16[4096,512]{1,0:T(8,128)(2,1)} async-done(((bf16[128,512]{1,0:T(8,128)(2,1)}), bf16[4096,512]{1,0:T(8,128)(2,1)}) %all-gather.12.cloned.1.call-update) | async-done | bytes 4194320 | tf_op jit(solution)/shard_map/all_gather | solution.py:72
  547.7 3.6 convolution_convert_fusion.3
  551.2 0.0 all-gather.14.cloned.1.call-update
  551.3 38.9 %all-gather.14.cloned.1.call-done = bf16[1024,512]{1,0:T(8,128)(2,1)} async-done(((bf16[128,512]{1,0:T(8,128)(2,1)}), bf16[1024,512]{1,0:T(8,128)(2,1)}) %all-gather.14.cloned.1.call-update) | async-done | bytes 1048592 | tf_op jit(solution)/shard_map/all_gather | solution.py:38
  590.2 4.8 collective-permute-start
  595.1 1.3 convolution_convert_fusion.2
  596.4 0.1 copy.19
  596.5 40.4 %collective-permute-done = bf16[1024,512]{1,0:T(8,128)(2,1)} collective-permute-done((bf16[1024,512]{1,0:T(8,128)(2,1)}, bf16[1024,512]{1,0:T(8,128)(2,1)}, u32[]{:S(2)}, u32[]{:S(2)}) %collective-permute-start) | collective-permute-done | bytes 1048608 | tf_op jit(solution)/shard_map/ppermute | solution.py:15
  636.9 2.8 convolution_convert_fusion
  639.7 0.0 copy-done.2
  639.7 1.1 fusion.31
  640.9 4.6 fusion.33
  645.5 0.0 copy-start.3
  645.5 3.1 fusion.21
  648.6 0.0 copy-done
  648.6 0.0 copy-done.3
  648.6 0.9 fusion.20
  (2 shorter events, 0.0 us)
Async XLA Ops:
  7.2 641.4 %copy-start = (bf16[512,512]{1,0:T(8,128)(2,1)S(1)}, bf16[512,512]{1,0:T(8,128)(2,1)}, u32[]{:S(2)}) copy-start(bf16[512,512]{1,0:T(8,128)(2,1)} %param.15) | copy-start | bytes 1572868
  7.2 100.4 %all-gather.8.cloned.1.call-start = ((), (), s32[]{:S(2)}) async-start(), calls=%async_computation.2 | async-start | bytes 6488064 | tf_op jit(solution)/shard_map/all_gather | solution.py:53
  7.9 193.6 %all-gather.6.cloned.1.call-start = ((), (), s32[]{:S(2)}) async-start(), calls=%async_computation.1 | async-start | bytes 9437184 | tf_op jit(solution)/shard_map/all_gather | solution.py:48
  13.8 265.9 %all-gather.10.cloned.1.call-start = ((), (), s32[]{:S(2)}) async-start(), calls=%async_computation.3 | async-start | bytes 2162688 | tf_op jit(solution)/shard_map/all_gather | solution.py:64
  14.5 445.4 %reduce-scatter.2.cloned.1.call-start = ((), (), s32[]{:S(2)}) async-start(), calls=%async_computation.4 | async-start | bytes 18874368 | tf_op jit(solution)/shard_map/reduce_scatter | solution.py:67
  289.4 170.6 %copy-start.1 = (bf16[128,4096]{1,0:T(8,128)(2,1)S(1)}, bf16[128,4096]{1,0:T(8,128)(2,1)}, u32[]{:S(2)}) copy-start(bf16[128,4096]{1,0:T(8,128)(2,1)} %param.8) | copy-start | bytes 3145732
  289.4 258.3 %all-gather.12.cloned.1.call-start = ((), (), s32[]{:S(2)}) async-start(), calls=%async_computation.5 | async-start | bytes 4325376 | tf_op jit(solution)/shard_map/all_gather | solution.py:72
  290.0 300.2 %all-gather.14.cloned.1.call-start = ((), (), s32[]{:S(2)}) async-start(), calls=%async_computation.6 | async-start | bytes 1179648 | tf_op jit(solution)/shard_map/all_gather | solution.py:38
  461.8 177.9 %copy-start.2 = (bf16[128,4096]{1,0:T(8,128)(2,1)}, bf16[128,4096]{1,0:T(8,128)(2,1)S(1)}, u32[]{:S(2)}) copy-start(bf16[128,4096]{1,0:T(8,128)(2,1)S(1)} %fusion.16) | copy-start | bytes 3145732
  590.2 46.7 %collective-permute-start = (bf16[1024,512]{1,0:T(8,128)(2,1)}, bf16[1024,512]{1,0:T(8,128)(2,1)}, u32[]{:S(2)}, u32[]{:S(2)}) collective-permute-start(bf16[1024,512]{1,0:T(8,128)(2,1)} %all-gather.14.cloned.1.call-done), channel_id=1, source_target_pairs={{128,0},{136,8},{144,16},{152,24},{160,32},{168,40},{176,48},{184,... | collective-permute-start | bytes 3145736 | tf_op jit(solution)/shard_map/ppermute | solution.py:15
  645.5 3.2 copy-start.3
Sparse Core Ops, SparseCore 0:
  10.8 96.7 all-gather.7
  110.0 91.4 all-gather.5
  204.1 75.5 all-gather.9
  289.5 170.4 reduce-scatter.1
  462.6 85.0 all-gather.11
  551.4 38.7 all-gather.13
where the time goes:
time: 657 us; the launch traced here: 656 us
  waiting for transfers between devices  582 us (89%)
  matrix products  46.1 us (7%)
  between operations  14.2 us (2%)
  other arithmetic  7.61 us (1%)
    reduce_scatter x1, waiting for transfers between devices, per_device(): lax.psum_scatter(head_terms, 'tensor', scatter_dimension=0, tiled=True)  170 us
    all_gather x1, waiting for transfers between devices, per_device(): all_normed = lax.all_gather(normed, 'tensor', axis=0, tiled=True)  93.9 us
    all_gather x1, waiting for transfers between devices, per_device(): lax.all_gather(qkv_weight, 'dp', axis=0, tiled=True)  93 us
    all_gather x1, waiting for transfers between devices, per_device(): lax.all_gather(match_weight, 'dp', axis=0, tiled=True)  85.9 us
    all_gather x1, waiting for transfers between devices, per_device(): lax.all_gather(out_weight, 'dp', axis=1, tiled=True)  58.1 us
    ppermute x1, waiting for transfers between devices, shifted(): return lax.ppermute(block, axis, route)  40.4 us
    all_gather x1, waiting for transfers between devices, relay(): whole_image = lax.all_gather(sending, 'tensor', axis=0, tiled=True)  38.9 us
  transfers between devices with their start and end apart: 7, of which 7 were waited for; matrix products, arithmetic and copies ran while one was open for 4% of the time, Pallas kernels for 0%

commit v1 on v0

v1 whole, which is shorter than its diff:
```python
import itertools
import math

import jax
import jax.numpy as jnp
from jax import lax
from jax.sharding import Mesh
from jax.sharding import PartitionSpec as P

HEAD_DIM = 128
MATCH_HEADS = 8
AXES = ("z", "xh", "core", "xl", "y")
SIZES = (8, 2, 2, 2, 4)


def moved(block, target):
    def index(place):
        at = 0
        for axis, size in zip(AXES, SIZES):
            at = at * size + place[axis]
        return at

    route = []
    for values in itertools.product(*[range(size) for size in SIZES]):
        place = dict(zip(AXES, values))
        route.append((index(place), index({**place, **target(place)})))
    return lax.ppermute(block, AXES, route)


def along_y(k):
    return lambda p: {"y": (p["y"] + k) % 4}


def along_z(k):
    return lambda p: {"z": (p["z"] + k) % 8}


def along_x(k):
    def target(p):
        x = (p["xh"] * 2 + p["xl"] + k) % 4
        return {"xh": x // 2, "xl": x % 2}

    return target


def other_core(p):
    return {"core": 1 - p["core"]}


def swapped_roles(block):
    return moved(block, lambda p: {"core": p["xl"], "xl": p["core"]})


def ring(block, step, count):
    half = block.shape[0] // 2
    up = down = block
    found = [(0, 0, block)]
    for s in range(1, count // 2):
        up, down = moved(up, step(1)), moved(down, step(-1))
        found += [(-s, 0, up), (s, 0, down)]
    found.append((-(count // 2), 0, moved(up[:half], step(1))))
    found.append((count // 2, half, moved(down[half:], step(-1))))
    return found


def layer_norm(rows_in, norm_gain, norm_bias):
    values = rows_in.astype(jnp.float32)
    center = jnp.mean(values, axis=-1, keepdims=True)
    spread = jnp.mean((values - center) ** 2, axis=-1, keepdims=True)
    return ((values - center) * lax.rsqrt(spread + 1e-06) * norm_gain + norm_bias).astype(
        jnp.bfloat16
    )


def attend_tokens(queries, keys, values, score_scale):
    scores = (
        jnp.einsum("qhd,khd->hqk", queries, keys, preferred_element_type=jnp.float32) * score_scale
    )
    probs = jax.nn.softmax(scores, axis=-1).astype(jnp.bfloat16)
    mixed_output = jnp.einsum("hqk,khd->qhd", probs, values, preferred_element_type=jnp.float32)
    return mixed_output.astype(jnp.bfloat16)


def per_device(
    tokens, norm_gain, norm_bias, qkv_weight, out_weight, match_weight, matcher_qkv, matcher_out
):
    bf16, f32 = jnp.bfloat16, jnp.float32
    z, y, core = lax.axis_index("z"), lax.axis_index("y"), lax.axis_index("core")
    x = lax.axis_index("xh") * 2 + lax.axis_index("xl")
    width = matcher_out.shape[0]
    rows, features_width = tokens.shape

    tokens = swapped_roles(tokens)
    qkv_weight = swapped_roles(qkv_weight)
    out_weight = swapped_roles(out_weight)

    normed = layer_norm(tokens, norm_gain, norm_bias)
    all_normed = lax.all_gather(normed, ("core", "y"), axis=0, tiled=True)

    block = qkv_weight.shape[0]
    columns = qkv_weight.shape[1]
    half = columns // 2
    weights = jnp.zeros((8, 4, block, columns), bf16)
    by_x = jnp.zeros((4, block, half), bf16)
    for dx, first, part in ring(qkv_weight[:, :half], along_x, 4):
        by_x = lax.dynamic_update_slice(by_x, part[None], ((x + dx) % 4, first, 0))
    by_z = jnp.zeros((8, block, half), bf16)
    for dz, first, part in ring(qkv_weight[:, half:], along_z, 8):
        by_z = lax.dynamic_update_slice(by_z, part[None], ((z + dz) % 8, first, 0))
    for dz, first, part in ring(by_x, along_z, 8):
        weights = lax.dynamic_update_slice(weights, part[None], ((z + dz) % 8, first, 0, 0))
    for dx, first, part in ring(by_z, along_x, 4):
        weights = lax.dynamic_update_slice(
            weights, part[:, None], (first, (x + dx) % 4, 0, half)
        )
    weights = weights.reshape(32 * block, columns)

    projected = jnp.dot(all_normed, weights, preferred_element_type=f32).astype(bf16)
    local_heads = columns // (3 * HEAD_DIM)
    patch_count = projected.shape[0]
    projected = projected.reshape(patch_count, local_heads, 3, HEAD_DIM)
    attended = attend_tokens(
        projected[:, :, 0], projected[:, :, 1], projected[:, :, 2], 1.0 / math.sqrt(HEAD_DIM)
    )
    attended = attended.reshape(2, patch_count // 2, local_heads * HEAD_DIM)

    out_z = jnp.zeros((8, 1, out_weight.shape[0], out_weight.shape[1]), bf16)
    for dz, first, part in ring(out_weight, along_z, 8):
        out_z = lax.dynamic_update_slice(out_z, part[None, None], ((z + dz) % 8, 0, first, 0))
    out_own = jnp.zeros((8, 4, out_weight.shape[0], out_weight.shape[1]), bf16)
    for dx, first, part in ring(out_z, along_x, 4):
        out_own = lax.dynamic_update_slice(out_own, part, (first, (x + dx) % 4, 0, 0))
    out_own = out_own.reshape(32, out_weight.shape[0], out_weight.shape[1])
    out_own = out_own.transpose(1, 0, 2).reshape(out_weight.shape[0], features_width)
    out_both = jnp.concatenate([out_own, moved(out_own, other_core)], axis=0)

    mine = lax.dynamic_index_in_dim(attended, core, 0, keepdims=False)
    theirs = lax.dynamic_index_in_dim(attended, 1 - core, 0, keepdims=False)
    both = jnp.concatenate([mine, moved(theirs, other_core)], axis=1)

    def term(dy):
        start = ((y + dy) % 4) * rows
        picked = lax.dynamic_slice_in_dim(both, start, rows, axis=0)
        return jnp.dot(picked, out_both, preferred_element_type=f32)

    far = term(2).astype(bf16)
    mid = rows // 2
    far_up = moved(far[:mid], along_y(1))
    far_down = moved(far[mid:], along_y(-1))
    near_up, near_down = term(1), term(-1)
    near_up = jnp.concatenate([near_up[:mid] + far_up.astype(f32), near_up[mid:]], axis=0)
    near_down = jnp.concatenate([near_down[:mid], near_down[mid:] + far_down.astype(f32)], axis=0)
    from_below = moved(near_up.astype(bf16), along_y(1))
    from_above = moved(near_down.astype(bf16), along_y(-1))
    summed = term(0) + from_below.astype(f32) + from_above.astype(f32)
    features = (tokens.astype(f32) + summed).astype(bf16)

    other_half = moved(
        match_weight, lambda p: {"xh": 1 - p["xh"], "xl": 1 - p["xl"]}
    )
    xh = lax.axis_index("xh")
    match_pair = jnp.where(
        xh == 0,
        jnp.concatenate([match_weight, other_half], axis=0),
        jnp.concatenate([other_half, match_weight], axis=0),
    ).reshape(2, 1, match_weight.shape[0], width)
    match_all = lax.all_gather(match_pair, ("z", "core"), axis=0, tiled=False)
    match_all = match_all.reshape(8, 2, 2, match_weight.shape[0], width)
    match_all = match_all.transpose(0, 2, 1, 3, 4).reshape(features_width, width)

    descriptor = jnp.dot(features, match_all, preferred_element_type=f32).astype(bf16)
    partner = moved(descriptor, along_z(4))
    matcher_queries = jnp.dot(
        descriptor, matcher_qkv[:, :width], preferred_element_type=f32
    ).astype(bf16)
    quarter = jnp.concatenate([partner] + [moved(partner, along_y(k)) for k in (1, 2, 3)], axis=0)
    partner_rows = jnp.concatenate([quarter, moved(quarter, other_core)], axis=0)
    key_values = jnp.dot(partner_rows, matcher_qkv[:, width:], preferred_element_type=f32).astype(
        bf16
    )
    key_count = key_values.shape[0]
    head_width = width // MATCH_HEADS
    mixed_output = attend_tokens(
        matcher_queries.reshape(rows, MATCH_HEADS, head_width),
        key_values[:, :width].reshape(key_count, MATCH_HEADS, head_width),
        key_values[:, width:].reshape(key_count, MATCH_HEADS, head_width),
        1.0 / math.sqrt(head_width),
    )
    mixed_output = mixed_output.reshape(rows, width)
    matched = descriptor.astype(f32) + jnp.dot(
        mixed_output, matcher_out, preferred_element_type=f32
    )
    return (swapped_roles(features), swapped_roles(matched.astype(bf16)))


def solution(mesh):
    fine = Mesh(mesh.devices.reshape(SIZES), AXES)
    dp, tensor = ("z", "xh", "core"), ("xl", "y")
    return jax.shard_map(
        per_device,
        mesh=fine,
        in_specs=(
            P(AXES, None),
            P(),
            P(),
            P(dp, tensor),
            P(tensor, dp),
            P(dp, None),
            P(),
            P(),
        ),
        out_specs=(P(AXES, None), P(AXES, None)),
        check_vma=False,
    )
```

time: 657 us -> 312 us (0.47)
  the two profiles are of different devices: /device:TPU:32 before, /device:TPU:1 now
where the time goes in v1:
time: 312 us; the launch traced here: 310 us
  starting transfers between devices  108 us (35%)
  waiting for transfers between devices  87.6 us (28%)
  matrix products  49.5 us (16%)
  local copies, waits for them, and re-layouts  43.6 us (14%)
  between operations  15.3 us (5%)
  other arithmetic  5.79 us (2%)
    ppermute x53, starting transfers between devices, moved(): return lax.ppermute(block, AXES, route)  108 us
    ppermute x53, waiting for transfers between devices, moved(): return lax.ppermute(block, AXES, route)  87.6 us
    dot_general x4, matrix products, term(): return jnp.dot(picked, out_both, preferred_element_type=f32)  15.7 us
    dot_general x1, matrix products, per_device(): jnp.dot(all_normed, weights, preferred_element_type=f32).astype(bf16)  11 us
    sub x2, matrix products, attend_tokens(): probs = jax.nn.softmax(scores, axis=-1).astype(jnp.bfloat16)  9.64 us
    dot_general x2, matrix products, attend_tokens(): jnp.einsum('hqk,khd->qhd', probs, values, preferred_element_type=jnp.floa...  7.74 us
    dynamic_update_slice x9, local copies, waits for them, and re-layouts, per_device(): lax.dynamic_update_slice(weights, part[None], ((z + dz) % 8, first, 0, 0))  7.16 us
  transfers between devices with their start and end apart: 55, of which 18 were waited for; matrix products, arithmetic and copies ran while one was open for 28% of the time, Pallas kernels for 0%

profile of v1, /device:TPU:1, one launch (start us, length us, event | category | flops | bytes accessed | tf_op | source)
XLA Modules:
  0.0 309.6 jit_solution(18316237407326513828)
XLA Ops:
  7.3 4.6 %collective-permute-start = (bf16[128,4096]{1,0:T(8,128)(2,1)}, bf16[128,4096]{1,0:T(8,128)(2,1)S(1)}, u32[]{:S(2)}, u32[]{:S(2)}) collective-permute-start(bf16[128,4096]{1,0:T(8,128)(2,1)} %param.8), channel_id=1, source_target_pairs={{0,0},{1,1},{2,2},{3,3},{4,8},{5,9},{6,10},{7,11},{8,4},{9,5},{10,... | collective-permute-start | bytes 3145736 | tf_op jit(solution)/shard_map/ppermute | solution.py:27
  11.9 12.7 %collective-permute-done = bf16[128,4096]{1,0:T(8,128)(2,1)S(1)} collective-permute-done((bf16[128,4096]{1,0:T(8,128)(2,1)}, bf16[128,4096]{1,0:T(8,128)(2,1)S(1)}, u32[]{:S(2)}, u32[]{:S(2)}) %collective-permute-start) | collective-permute-done | bytes 1048608 | tf_op jit(solution)/shard_map/ppermute | solution.py:27
  25.3 2.2 fusion.18
  27.5 3.6 %collective-permute-start.27 = (bf16[256,128]{1,0:T(8,128)(2,1)S(1)}, bf16[256,128]{1,0:T(8,128)(2,1)S(1)}, u32[]{:S(2)}, u32[]{:S(2)}) collective-permute-start(bf16[256,128]{1,0:T(8,128)(2,1)S(1)} %copy-done.11), channel_id=1, source_target_pairs={{0,0},{1,1},{2,2},{3,3},{4,8},{5,9},{6,10},{7,11},{8,4},{9,5},{10,... | collective-permute-start | bytes 196616 | tf_op jit(solution)/shard_map/ppermute | solution.py:27
  31.3 1.9 collective-permute-start.1
  33.6 1.7 collective-permute-start.28
  35.3 4.0 %collective-permute-start.29 = (bf16[256,128]{1,0:T(8,128)(2,1)S(1)}, bf16[256,128]{1,0:T(8,128)(2,1)S(1)}, u32[]{:S(2)}, u32[]{:S(2)}) collective-permute-start(bf16[256,128]{1,0:T(8,128)(2,1)S(1)} %collective-permute-done.27), channel_id=1, source_target_pairs={{0,224},{1,225},{2,226},{3,227},{4,228},{5,229},{6,230},{7,231},{8... | collective-permute-start | bytes 196616 | tf_op jit(solution)/shard_map/ppermute | solution.py:27
  39.4 1.5 collective-permute-done.28
  42.1 2.7 collective-permute-start.31
  44.8 1.7 collective-permute-done.30
  48.4 1.5 collective-permute-start.32
  49.9 1.3 collective-permute-start.33
  52.7 1.8 collective-permute-start.3
  57.3 1.5 collective-permute-start.34
  59.4 1.2 collective-permute-start.35
  61.7 10.2 %collective-permute-start.15 = (bf16[128,384]{1,0:T(8,128)(2,1)}, bf16[128,384]{1,0:T(8,128)(2,1)S(1)}, u32[]{:S(2)}, u32[]{:S(2)}) collective-permute-start(bf16[128,384]{1,0:T(8,128)(2,1)} %get-tuple-element.8), channel_id=1, source_target_pairs={{0,224},{1,225},{2,226},{3,227},{4,228},{5,229},{6,230},{7,231},{8... | collective-permute-start | bytes 294920 | tf_op jit(solution)/shard_map/ppermute | solution.py:27
  72.4 1.6 broadcast_in_dim.165
  74.8 2.7 collective-permute-start.37
  81.0 2.7 collective-permute-start.5
  84.8 2.7 collective-permute-start.17
  87.6 3.4 %broadcast_in_dim.134 = bf16[8,4,128,768]{3,2,1,0:T(8,128)(2,1)} broadcast(bf16[]{:T(256)} %constant.190.clone.1), dimensions={} | broadcast | bytes 6291458 | tf_op jit(solution)/shard_map/broadcast_in_dim | solution.py:103
  91.8 2.7 collective-permute-start.7
  94.7 6.9 %collective-permute-done.18 = bf16[128,384]{1,0:T(8,128)(2,1)S(1)} collective-permute-done((bf16[128,384]{1,0:T(8,128)(2,1)S(1)}, bf16[128,384]{1,0:T(8,128)(2,1)S(1)}, u32[]{:S(2)}, u32[]{:S(2)}) %collective-permute-start.18) | collective-permute-done | bytes 98336 | tf_op jit(solution)/shard_map/ppermute | solution.py:27
  101.6 6.9 %collective-permute-done.19 = bf16[128,384]{1,0:T(8,128)(2,1)S(1)} collective-permute-done((bf16[128,384]{1,0:T(8,128)(2,1)S(1)}, bf16[128,384]{1,0:T(8,128)(2,1)S(1)}, u32[]{:S(2)}, u32[]{:S(2)}) %collective-permute-start.19) | collective-permute-done | bytes 98336 | tf_op jit(solution)/shard_map/ppermute | solution.py:27
  108.6 6.1 %collective-permute-done.20 = bf16[64,384]{1,0:T(8,128)(2,1)S(1)} collective-permute-done((bf16[64,384]{1,0:T(8,128)(2,1)S(1)}, bf16[64,384]{1,0:T(8,128)(2,1)S(1)}, u32[]{:S(2)}, u32[]{:S(2)}) %collective-permute-start.20) | collective-permute-done | bytes 49184 | tf_op jit(solution)/shard_map/ppermute | solution.py:27
  115.4 3.6 %collective-permute-done.21 = bf16[64,384]{1,0:T(8,128)(2,1)S(1)} collective-permute-done((bf16[64,384]{1,0:T(8,128)(2,1)S(1)}, bf16[64,384]{1,0:T(8,128)(2,1)S(1)}, u32[]{:S(2)}, u32[]{:S(2)}) %collective-permute-start.21) | collective-permute-done | bytes 49184 | tf_op jit(solution)/shard_map/ppermute | solution.py:27
  119.8 2.2 collective-permute-start.9
  123.8 2.7 collective-permute-start.39
  127.4 6.5 %collective-permute-done.38 = bf16[4,1,256,128]{2,3,1,0:T(8,128)(2,1)S(1)} collective-permute-done((bf16[4,1,256,128]{2,3,1,0:T(8,128)(2,1)S(1)}, bf16[4,1,256,128]{2,3,1,0:T(8,128)(2,1)S(1)}, u32[]{:S(2)}, u32[]{:S(2)}) %collective-permute-start.38) | collective-permute-done | bytes 262176 | tf_op jit(solution)/shard_map/ppermute | solution.py:27
  136.2 14.8 %collective-permute-start.40 = (bf16[256,4096]{0,1:T(8,128)(2,1)}, bf16[256,4096]{0,1:T(8,128)(2,1)}, u32[]{:S(2)}, u32[]{:S(2)}) collective-permute-start(bf16[256,4096]{0,1:T(8,128)(2,1)} %bitcast.51), channel_id=1, source_target_pairs={{0,8},{1,9},{2,10},{3,11},{4,12},{5,13},{6,14},{7,15},{8,0},{9,1},... | collective-permute-start | bytes 6291464 | tf_op jit(solution)/shard_map/ppermute | solution.py:27
  151.0 2.7 collective-permute-start.11
  155.3 1.8 collective-permute-start.24
  158.2 4.7 %collective-permute-done.10 = bf16[4,128,384]{2,1,0:T(8,128)(2,1)S(1)} collective-permute-done((bf16[4,128,384]{2,1,0:T(8,128)(2,1)S(1)}, bf16[4,128,384]{2,1,0:T(8,128)(2,1)S(1)}, u32[]{:S(2)}, u32[]{:S(2)}) %collective-permute-start.10) | collective-permute-done | bytes 393248 | tf_op jit(solution)/shard_map/ppermute | solution.py:27
  163.1 3.1 %collective-permute-start.13 = (bf16[2,128,384]{2,1,0:T(8,128)(2,1)S(1)}, bf16[2,128,384]{2,1,0:T(8,128)(2,1)S(1)}, u32[]{:S(2)}, u32[]{:S(2)}) collective-permute-start(bf16[2,128,384]{2,1,0:T(8,128)(2,1)S(1)} %slice.114), channel_id=1, source_target_pairs={{0,224},{1,225},{2,226},{3,227},{4,228},{5,229},{6,230},{7,231},{8... | collective-permute-start | bytes 589832 | tf_op jit(solution)/shard_map/ppermute | solution.py:27
  167.9 2.0 collective-permute-done.12
  176.1 11.0 %convolution_convert_fusion.2 = bf16[1024,768]{0,1:T(8,128)(2,1)S(1)} fusion(bf16[1024,4096]{1,0:T(8,128)(2,1)} %all-gather.3.cloned.1.call-done, bf16[4096,768]{1,0:T(8,128)(2,1)} %bitcast.32), kind=kOutput, calls=%fused_computation.29 | convolution fusion | flops 6443237376 | bytes 16252928 | tf_op jit(solution)/shard_map/dot_general | solution.py:118
  187.1 5.0 %fusion.57 = (f32[2,1024]{1,0:T(2,128)S(1)}, f32[2,1024,1024]{1,2,0:T(8,128)}) fusion(bf16[1024,2,3,128]{0,3,2,1:T(8,128)(2,1)S(1)} %bitcast.158), kind=kOutput, calls=%fused_computation.133 | convolution fusion | flops 543163392 | bytes 9445376 | tf_op jit(solution)/shard_map/sub | solution.py:79
  192.1 4.3 %fusion.22 = bf16[1024,2,128]{0,2,1:T(8,128)(2,1)S(1)} fusion(f32[2,1024,1024]{1,2,0:T(8,128)} %get-tuple-element.13, f32[2,1024]{1,0:T(2,128)S(1)} %get-tuple-element.12, bf16[1024,2,3,128]{0,3,2,1:T(8,128)(2,1)} %bitcast.159), kind=kOutput, calls=%fused_computation.31 | convolution fusion | flops 541327360 | bytes 9445376 | tf_op jit(solution)/shard_map/hqk,khd->qhd/dot_general | solution.py:80
  198.4 1.8 collective-permute-start.26
  201.3 3.8 %convolution_convert_fusion = bf16[128,4096]{1,0:T(8,128)(2,1)S(1)} fusion(s32[]{:T(128)S(6)} %select_n.273, bf16[512,256]{1,0:T(8,128)(2,1)S(1)} %bitcast.144, bf16[512,256]{1,0:T(8,128)(2,1)S(1)} %collective-permute-done.26, bf16[256,4096]{0,1:T(8,128)(2,1)} %collective-permute-done.40, bf16[256,4096]{0,1:T(8,128)(2,1)} %bitcast.51), kind=kOutput, calls=%fused_computation.10 | convolution fusion | flops 546045952 | bytes 5767172 | tf_op jit(solution)/shard_map/dot_general | solution.py:144
  205.2 1.5 collective-permute-start.41
  206.7 3.8 %fusion.40 = f32[128,4096]{1,0:T(8,128)S(1)} fusion(s32[]{:T(128)S(6)} %select_n.271, bf16[512,256]{1,0:T(8,128)(2,1)S(1)} %bitcast.145, bf16[512,256]{1,0:T(8,128)(2,1)} %copy-done.7, bf16[256,4096]{0,1:T(8,128)(2,1)} %collective-permute-done.40, bf16[256,4096]{0,1:T(8,128)(2,1)} %bitcast.51), kind=kOutput, calls=%fused_computation.81 | convolution fusion | flops 545521664 | bytes 6815748 | tf_op jit(solution)/shard_map/dot_general | solution.py:144
  210.6 1.5 collective-permute-start.43
  212.0 3.7 %fusion.35 = f32[128,4096]{1,0:T(8,128)S(1)} fusion(s32[]{:T(128)S(6)} %select_n.275, bf16[512,256]{1,0:T(8,128)(2,1)S(1)} %bitcast.146, bf16[512,256]{1,0:T(8,128)(2,1)S(1)} %copy-done.8, bf16[256,4096]{0,1:T(8,128)(2,1)} %collective-permute-done.40, bf16[256,4096]{0,1:T(8,128)(2,1)} %bitcast.51), kind=kOutput, calls=%fused_computation.78 | convolution fusion | flops 545521664 | bytes 6815748 | tf_op jit(solution)/shard_map/dot_general | solution.py:144
  215.8 3.8 %collective-permute-done.41 = bf16[64,4096]{1,0:T(8,128)(2,1)S(1)} collective-permute-done((bf16[64,4096]{1,0:T(8,128)(2,1)S(1)}, bf16[64,4096]{1,0:T(8,128)(2,1)S(1)}, u32[]{:S(2)}, u32[]{:S(2)}) %collective-permute-start.41) | collective-permute-done | bytes 524320 | tf_op jit(solution)/shard_map/ppermute | solution.py:27
  220.1 3.5 %collective-permute-done.43 = bf16[64,4096]{1,0:T(8,128)(2,1)S(1)} collective-permute-done((bf16[64,4096]{1,0:T(8,128)(2,1)S(1)}, bf16[64,4096]{1,0:T(8,128)(2,1)S(1)}, u32[]{:S(2)}, u32[]{:S(2)}) %collective-permute-start.43) | collective-permute-done | bytes 524320 | tf_op jit(solution)/shard_map/ppermute | solution.py:27
  224.8 2.4 collective-permute-start.44
  227.2 2.7 copy.75
  229.9 14.7 %collective-permute-done.42 = bf16[128,4096]{1,0:T(8,128)(2,1)} collective-permute-done((bf16[128,4096]{1,0:T(8,128)(2,1)S(1)}, bf16[128,4096]{1,0:T(8,128)(2,1)}, u32[]{:S(2)}, u32[]{:S(2)}) %collective-permute-start.42) | collective-permute-done | bytes 1048608 | tf_op jit(solution)/shard_map/ppermute | solution.py:27
  244.6 3.8 %collective-permute-done.44 = bf16[128,4096]{1,0:T(8,128)(2,1)} collective-permute-done((bf16[128,4096]{1,0:T(8,128)(2,1)}, bf16[128,4096]{1,0:T(8,128)(2,1)}, u32[]{:S(2)}, u32[]{:S(2)}) %collective-permute-start.44) | collective-permute-done | bytes 1048608 | tf_op jit(solution)/shard_map/ppermute | solution.py:27
  248.5 4.4 %fusion.7 = bf16[128,4096]{1,0:T(8,128)(2,1)S(1)} fusion(bf16[128,4096]{1,0:T(8,128)(2,1)S(1)} %collective-permute-done, bf16[128,4096]{1,0:T(8,128)(2,1)} %collective-permute-done.44, bf16[128,4096]{1,0:T(8,128)(2,1)} %collective-permute-done.42, s32[]{:T(128)S(6)} %select_n.269, bf16[512,256]{1,0:T(8,128)(2,1)S(1)} %bitcast.147, ...), kind=kOutput, calls=%fused_computation.9 | convolution fusion | flops 549191680 | bytes 8912900 | tf_op jit(solution)/shard_map/dot_general | solution.py:144
  253.6 4.7 %collective-permute-start.47 = (bf16[128,512]{1,0:T(8,128)(2,1)S(1)}, bf16[128,512]{1,0:T(8,128)(2,1)S(1)}, u32[]{:S(2)}, u32[]{:S(2)}) collective-permute-start(bf16[128,512]{1,0:T(8,128)(2,1)S(1)} %convolution_convert_fusion.4), channel_id=1, source_target_pairs={{0,128},{1,129},{2,130},{3,131},{4,132},{5,133},{6,134},{7,135},{8... | collective-permute-start | bytes 393224 | tf_op jit(solution)/shard_map/ppermute | solution.py:27
  258.3 4.5 %collective-permute-done.47 = bf16[128,512]{1,0:T(8,128)(2,1)S(1)} collective-permute-done((bf16[128,512]{1,0:T(8,128)(2,1)S(1)}, bf16[128,512]{1,0:T(8,128)(2,1)S(1)}, u32[]{:S(2)}, u32[]{:S(2)}) %collective-permute-start.47) | collective-permute-done | bytes 131104 | tf_op jit(solution)/shard_map/ppermute | solution.py:27
  263.8 3.6 %collective-permute-start.49 = (bf16[128,512]{1,0:T(8,128)(2,1)S(1)}, bf16[128,512]{1,0:T(8,128)(2,1)S(1)}, u32[]{:S(2)}, u32[]{:S(2)}) collective-permute-start(bf16[128,512]{1,0:T(8,128)(2,1)S(1)} %collective-permute-done.47), channel_id=1, source_target_pairs={{0,2},{1,3},{2,0},{3,1},{4,6},{5,7},{6,4},{7,5},{8,10},{9,11},{10,... | collective-permute-start | bytes 393224 | tf_op jit(solution)/shard_map/ppermute | solution.py:27
  267.4 7.2 %collective-permute-start.45 = (bf16[128,4096]{1,0:T(8,128)(2,1)S(1)}, bf16[128,4096]{1,0:T(8,128)(2,1)S(1)}, u32[]{:S(2)}, u32[]{:S(2)}) collective-permute-start(bf16[128,4096]{1,0:T(8,128)(2,1)S(1)} %fusion.7), channel_id=1, source_target_pairs={{0,0},{1,1},{2,2},{3,3},{4,8},{5,9},{6,10},{7,11},{8,4},{9,5},{10,... | collective-permute-start | bytes 3145736 | tf_op jit(solution)/shard_map/ppermute | solution.py:27
  276.2 1.4 collective-permute-start.51
  277.6 1.9 convolution_convert_fusion.3
  279.5 1.7 copy.76
  282.2 2.5 convolution_convert_fusion.1
  284.8 1.5 fusion.54
  286.3 4.6 %fusion.58 = (f32[8,128]{1,0:T(8,128)S(1)}, f32[8,128,1024]{2,1,0:T(8,128)}) fusion(bf16[128,8,64]{0,2,1:T(8,128)(2,1)S(1)} %bitcast.152, bf16[1024,8,64]{0,2,1:T(8,128)(2,1)} %bitcast.143), kind=kOutput, calls=%fused_computation.134 | convolution fusion | flops 137364480 | bytes 5378048 | tf_op jit(solution)/shard_map/sub | solution.py:79
  290.9 3.5 %fusion.24 = bf16[8,64,128]{2,1,0:T(8,128)(2,1)S(1)} fusion(bf16[1024,8,64]{0,2,1:T(8,128)(2,1)} %bitcast.142, f32[8,128,1024]{2,1,0:T(8,128)} %get-tuple-element.15, f32[8,128]{1,0:T(8,128)S(1)} %get-tuple-element.14), kind=kOutput, calls=%fused_computation.34 | convolution fusion | flops 136380416 | bytes 5378048 | tf_op jit(solution)/shard_map/hqk,khd->qhd/dot_general | solution.py:80
  294.7 3.5 %collective-permute-start.52 = (bf16[128,512]{1,0:T(8,128)(2,1)S(1)}, bf16[128,512]{1,0:T(8,128)(2,1)S(1)}, u32[]{:S(2)}, u32[]{:S(2)}) collective-permute-start(bf16[128,512]{1,0:T(8,128)(2,1)S(1)} %fusion.23), channel_id=1, source_target_pairs={{0,0},{1,1},{2,2},{3,3},{4,8},{5,9},{6,10},{7,11},{8,4},{9,5},{10,... | collective-permute-start | bytes 393224 | tf_op jit(solution)/shard_map/ppermute | solution.py:27
  298.2 2.8 collective-permute-done.52
  (183 shorter events, 45.0 us)
Async XLA Ops:
  7.2 287.2 %copy-start = (bf16[512,512]{1,0:T(8,128)(2,1)S(1)}, bf16[512,512]{1,0:T(8,128)(2,1)}, u32[]{:S(2)}) copy-start(bf16[512,512]{1,0:T(8,128)(2,1)} %param.15) | copy-start | bytes 1572868
  7.2 20.3 %copy-start.11 = (bf16[256,128]{1,0:T(8,128)(2,1)S(1)}, bf16[256,128]{1,0:T(8,128)(2,1)}, u32[]{:S(2)}) copy-start(bf16[256,128]{1,0:T(8,128)(2,1)} %param.12) | copy-start | bytes 196612
  7.2 24.0 %copy-start.5 = (bf16[128,512]{1,0:T(8,128)(2,1)S(1)}, bf16[128,512]{1,0:T(8,128)(2,1)}, u32[]{:S(2)}) copy-start(bf16[128,512]{1,0:T(8,128)(2,1)} %param.13) | copy-start | bytes 393220
  7.2 24.1 %copy-start.10 = (bf16[128,768]{1,0:T(8,128)(2,1)S(1)}, bf16[128,768]{1,0:T(8,128)(2,1)}, u32[]{:S(2)}) copy-start(bf16[128,768]{1,0:T(8,128)(2,1)} %param.11) | copy-start | bytes 589828
  7.2 168.9 %all-gather.3.cloned.1.call-start = ((), (), s32[]{:S(2)}) async-start(), calls=%async_computation | async-start | bytes 9437184 | tf_op jit(solution)/shard_map/all_gather | solution.py:98
  7.3 17.3 %collective-permute-start = (bf16[128,4096]{1,0:T(8,128)(2,1)}, bf16[128,4096]{1,0:T(8,128)(2,1)S(1)}, u32[]{:S(2)}, u32[]{:S(2)}) collective-permute-start(bf16[128,4096]{1,0:T(8,128)(2,1)} %param.8), channel_id=1, source_target_pairs={{0,0},{1,1},{2,2},{3,3},{4,8},{5,9},{6,10},{7,11},{8,4},{9,5},{10,... | collective-permute-start | bytes 3145736 | tf_op jit(solution)/shard_map/ppermute | solution.py:27
  27.5 199.7 %all-gather.5.cloned.1.call-start = ((), (), s32[]{:S(2)}) async-start(), calls=%async_computation.1 | async-start | bytes 4456448 | tf_op jit(solution)/shard_map/all_gather | solution.py:167
  27.5 6.0 %collective-permute-start.27 = (bf16[256,128]{1,0:T(8,128)(2,1)S(1)}, bf16[256,128]{1,0:T(8,128)(2,1)S(1)}, u32[]{:S(2)}, u32[]{:S(2)}) collective-permute-start(bf16[256,128]{1,0:T(8,128)(2,1)S(1)} %copy-done.11), channel_id=1, source_target_pairs={{0,0},{1,1},{2,2},{3,3},{4,8},{5,9},{6,10},{7,11},{8,4},{9,5},{10,... | collective-permute-start | bytes 196616 | tf_op jit(solution)/shard_map/ppermute | solution.py:27
  31.2 10.0 %collective-permute-start.46 = (bf16[128,512]{1,0:T(8,128)(2,1)S(1)}, bf16[128,512]{1,0:T(8,128)(2,1)S(1)}, u32[]{:S(2)}, u32[]{:S(2)}) collective-permute-start(bf16[128,512]{1,0:T(8,128)(2,1)S(1)} %copy-done.5), channel_id=1, source_target_pairs={{0,20},{1,21},{2,22},{3,23},{4,16},{5,17},{6,18},{7,19},{8,28},{9,... | collective-permute-start | bytes 393224 | tf_op jit(solution)/shard_map/ppermute | solution.py:27
  31.3 19.9 %collective-permute-start.1 = (bf16[128,768]{1,0:T(8,128)(2,1)S(1)}, bf16[128,768]{1,0:T(8,128)(2,1)S(1)}, u32[]{:S(2)}, u32[]{:S(2)}) collective-permute-start(bf16[128,768]{1,0:T(8,128)(2,1)S(1)} %copy-done.10), channel_id=1, source_target_pairs={{0,0},{1,1},{2,2},{3,3},{4,8},{5,9},{6,10},{7,11},{8,4},{9,5},{10,... | collective-permute-start | bytes 589832 | tf_op jit(solution)/shard_map/ppermute | solution.py:27
  33.6 7.3 %collective-permute-start.28 = (bf16[256,128]{1,0:T(8,128)(2,1)S(1)}, bf16[256,128]{1,0:T(8,128)(2,1)S(1)}, u32[]{:S(2)}, u32[]{:S(2)}) collective-permute-start(bf16[256,128]{1,0:T(8,128)(2,1)S(1)} %collective-permute-done.27), channel_id=1, source_target_pairs={{0,32},{1,33},{2,34},{3,35},{4,36},{5,37},{6,38},{7,39},{8,40},{9,... | collective-permute-start | bytes 196616 | tf_op jit(solution)/shard_map/ppermute | solution.py:27
  35.3 5.7 %collective-permute-start.29 = (bf16[256,128]{1,0:T(8,128)(2,1)S(1)}, bf16[256,128]{1,0:T(8,128)(2,1)S(1)}, u32[]{:S(2)}, u32[]{:S(2)}) collective-permute-start(bf16[256,128]{1,0:T(8,128)(2,1)S(1)} %collective-permute-done.27), channel_id=1, source_target_pairs={{0,224},{1,225},{2,226},{3,227},{4,228},{5,229},{6,230},{7,231},{8... | collective-permute-start | bytes 196616 | tf_op jit(solution)/shard_map/ppermute | solution.py:27
  42.0 4.5 %collective-permute-start.30 = (bf16[256,128]{1,0:T(8,128)(2,1)S(1)}, bf16[256,128]{1,0:T(8,128)(2,1)}, u32[]{:S(2)}, u32[]{:S(2)}) collective-permute-start(bf16[256,128]{1,0:T(8,128)(2,1)S(1)} %collective-permute-done.28), channel_id=1, source_target_pairs={{0,32},{1,33},{2,34},{3,35},{4,36},{5,37},{6,38},{7,39},{8,40},{9,... | collective-permute-start | bytes 196616 | tf_op jit(solution)/shard_map/ppermute | solution.py:27
  42.1 5.4 %collective-permute-start.31 = (bf16[256,128]{1,0:T(8,128)(2,1)S(1)}, bf16[256,128]{1,0:T(8,128)(2,1)}, u32[]{:S(2)}, u32[]{:S(2)}) collective-permute-start(bf16[256,128]{1,0:T(8,128)(2,1)S(1)} %collective-permute-done.29), channel_id=1, source_target_pairs={{0,224},{1,225},{2,226},{3,227},{4,228},{5,229},{6,230},{7,231},{8... | collective-permute-start | bytes 196616 | tf_op jit(solution)/shard_map/ppermute | solution.py:27
  48.4 6.5 %collective-permute-start.32 = (bf16[256,128]{1,0:T(8,128)(2,1)}, bf16[256,128]{1,0:T(8,128)(2,1)S(1)}, u32[]{:S(2)}, u32[]{:S(2)}) collective-permute-start(bf16[256,128]{1,0:T(8,128)(2,1)} %collective-permute-done.30), channel_id=1, source_target_pairs={{0,32},{1,33},{2,34},{3,35},{4,36},{5,37},{6,38},{7,39},{8,40},{9,... | collective-permute-start | bytes 196616 | tf_op jit(solution)/shard_map/ppermute | solution.py:27
  49.9 6.6 %collective-permute-start.33 = (bf16[256,128]{1,0:T(8,128)(2,1)}, bf16[256,128]{1,0:T(8,128)(2,1)S(1)}, u32[]{:S(2)}, u32[]{:S(2)}) collective-permute-start(bf16[256,128]{1,0:T(8,128)(2,1)} %collective-permute-done.31), channel_id=1, source_target_pairs={{0,224},{1,225},{2,226},{3,227},{4,228},{5,229},{6,230},{7,231},{8... | collective-permute-start | bytes 196616 | tf_op jit(solution)/shard_map/ppermute | solution.py:27
  51.9 22.9 %collective-permute-start.2 = (bf16[128,384]{1,0:T(8,128)(2,1)}, bf16[128,384]{1,0:T(8,128)(2,1)}, u32[]{:S(2)}, u32[]{:S(2)}) collective-permute-start(bf16[128,384]{1,0:T(8,128)(2,1)} %get-tuple-element.9), channel_id=1, source_target_pairs={{0,4},{1,5},{2,6},{3,7},{4,16},{5,17},{6,18},{7,19},{8,12},{9,13},... | collective-permute-start | bytes 294920 | tf_op jit(solution)/shard_map/ppermute | solution.py:27
  52.7 26.5 %collective-permute-start.3 = (bf16[128,384]{1,0:T(8,128)(2,1)}, bf16[128,384]{1,0:T(8,128)(2,1)}, u32[]{:S(2)}, u32[]{:S(2)}) collective-permute-start(bf16[128,384]{1,0:T(8,128)(2,1)} %get-tuple-element.9), channel_id=1, source_target_pairs={{0,20},{1,21},{2,22},{3,23},{4,0},{5,1},{6,2},{7,3},{8,28},{9,29},... | collective-permute-start | bytes 294920 | tf_op jit(solution)/shard_map/ppermute | solution.py:27
  54.5 26.4 %collective-permute-start.14 = (bf16[128,384]{1,0:T(8,128)(2,1)}, bf16[128,384]{1,0:T(8,128)(2,1)}, u32[]{:S(2)}, u32[]{:S(2)}) collective-permute-start(bf16[128,384]{1,0:T(8,128)(2,1)} %get-tuple-element.8), channel_id=1, source_target_pairs={{0,32},{1,33},{2,34},{3,35},{4,36},{5,37},{6,38},{7,39},{8,40},{9,... | collective-permute-start | bytes 294920 | tf_op jit(solution)/shard_map/ppermute | solution.py:27
  57.3 4.4 %collective-permute-start.34 = (bf16[128,128]{1,0:T(8,128)(2,1)S(1)}, bf16[128,128]{1,0:T(8,128)(2,1)S(1)}, u32[]{:S(2)}, u32[]{:S(2)}) collective-permute-start(bf16[128,128]{1,0:T(8,128)(2,1)S(1)} %slice.123), channel_id=1, source_target_pairs={{0,32},{1,33},{2,34},{3,35},{4,36},{5,37},{6,38},{7,39},{8,40},{9,... | collective-permute-start | bytes 98312 | tf_op jit(solution)/shard_map/ppermute | solution.py:27
  59.4 12.7 %collective-permute-start.35 = (bf16[128,128]{1,0:T(8,128)(2,1)}, bf16[128,128]{1,0:T(8,128)(2,1)S(1)}, u32[]{:S(2)}, u32[]{:S(2)}) collective-permute-start(bf16[128,128]{1,0:T(8,128)(2,1)} %slice.124), channel_id=1, source_target_pairs={{0,224},{1,225},{2,226},{3,227},{4,228},{5,229},{6,230},{7,231},{8... | collective-permute-start | bytes 98312 | tf_op jit(solution)/shard_map/ppermute | solution.py:27
  61.7 22.9 %collective-permute-start.15 = (bf16[128,384]{1,0:T(8,128)(2,1)}, bf16[128,384]{1,0:T(8,128)(2,1)S(1)}, u32[]{:S(2)}, u32[]{:S(2)}) collective-permute-start(bf16[128,384]{1,0:T(8,128)(2,1)} %get-tuple-element.8), channel_id=1, source_target_pairs={{0,224},{1,225},{2,226},{3,227},{4,228},{5,229},{6,230},{7,231},{8... | collective-permute-start | bytes 294920 | tf_op jit(solution)/shard_map/ppermute | solution.py:27
  72.3 50.6 %collective-permute-start.36 = (bf16[8,1,256,128]{2,3,1,0:T(8,128)(2,1)S(1)}, bf16[8,1,256,128]{2,3,1,0:T(8,128)(2,1)S(1)}, u32[]{:S(2)}, u32[]{:S(2)}) collective-permute-start(bf16[8,1,256,128]{2,3,1,0:T(8,128)(2,1)S(1)} %constant_dynamic-update-slice_fusion.5), channel_id=1, source_target_pairs={{0,4},{1,5},{2,6},{3,7},{4,16},{5,17},{6,18},{7,19},{8,12},{9,13},... | collective-permute-start | bytes 1572872 | tf_op jit(solution)/shard_map/ppermute | solution.py:27
  74.8 49.0 %collective-permute-start.37 = (bf16[8,1,256,128]{2,3,1,0:T(8,128)(2,1)S(1)}, bf16[8,1,256,128]{2,3,1,0:T(8,128)(2,1)S(1)}, u32[]{:S(2)}, u32[]{:S(2)}) collective-permute-start(bf16[8,1,256,128]{2,3,1,0:T(8,128)(2,1)S(1)} %constant_dynamic-update-slice_fusion.5), channel_id=1, source_target_pairs={{0,20},{1,21},{2,22},{3,23},{4,0},{5,1},{6,2},{7,3},{8,28},{9,29},... | collective-permute-start | bytes 1572872 | tf_op jit(solution)/shard_map/ppermute | solution.py:27
  79.2 5.6 %collective-permute-start.4 = (bf16[64,384]{1,0:T(8,128)(2,1)S(1)}, bf16[64,384]{1,0:T(8,128)(2,1)S(1)}, u32[]{:S(2)}, u32[]{:S(2)}) collective-permute-start(bf16[64,384]{1,0:T(8,128)(2,1)S(1)} %slice.111), channel_id=1, source_target_pairs={{0,4},{1,5},{2,6},{3,7},{4,16},{5,17},{6,18},{7,19},{8,12},{9,13},... | collective-permute-start | bytes 147464 | tf_op jit(solution)/shard_map/ppermute | solution.py:27
  81.0 6.5 %collective-permute-start.5 = (bf16[64,384]{1,0:T(8,128)(2,1)S(1)}, bf16[64,384]{1,0:T(8,128)(2,1)S(1)}, u32[]{:S(2)}, u32[]{:S(2)}) collective-permute-start(bf16[64,384]{1,0:T(8,128)(2,1)S(1)} %slice.112), channel_id=1, source_target_pairs={{0,20},{1,21},{2,22},{3,23},{4,0},{5,1},{6,2},{7,3},{8,28},{9,29},... | collective-permute-start | bytes 147464 | tf_op jit(solution)/shard_map/ppermute | solution.py:27
  84.6 7.2 %collective-permute-start.16 = (bf16[128,384]{1,0:T(8,128)(2,1)}, bf16[128,384]{1,0:T(8,128)(2,1)S(1)}, u32[]{:S(2)}, u32[]{:S(2)}) collective-permute-start(bf16[128,384]{1,0:T(8,128)(2,1)} %collective-permute-done.14), channel_id=1, source_target_pairs={{0,32},{1,33},{2,34},{3,35},{4,36},{5,37},{6,38},{7,39},{8,40},{9,... | collective-permute-start | bytes 294920 | tf_op jit(solution)/shard_map/ppermute | solution.py:27
  84.8 9.8 %collective-permute-start.17 = (bf16[128,384]{1,0:T(8,128)(2,1)S(1)}, bf16[128,384]{1,0:T(8,128)(2,1)S(1)}, u32[]{:S(2)}, u32[]{:S(2)}) collective-permute-start(bf16[128,384]{1,0:T(8,128)(2,1)S(1)} %collective-permute-done.15), channel_id=1, source_target_pairs={{0,224},{1,225},{2,226},{3,227},{4,228},{5,229},{6,230},{7,231},{8... | collective-permute-start | bytes 294920 | tf_op jit(solution)/shard_map/ppermute | solution.py:27
  87.5 31.5 %collective-permute-start.6 = (bf16[4,128,384]{2,1,0:T(8,128)(2,1)S(1)}, bf16[4,128,384]{2,1,0:T(8,128)(2,1)S(1)}, u32[]{:S(2)}, u32[]{:S(2)}) collective-permute-start(bf16[4,128,384]{2,1,0:T(8,128)(2,1)S(1)} %bitcast_dynamic-update-slice_fusion.26), channel_id=1, source_target_pairs={{0,32},{1,33},{2,34},{3,35},{4,36},{5,37},{6,38},{7,39},{8,40},{9,... | collective-permute-start | bytes 1179656 | tf_op jit(solution)/shard_map/ppermute | solution.py:27
  91.8 28.0 %collective-permute-start.7 = (bf16[4,128,384]{2,1,0:T(8,128)(2,1)S(1)}, bf16[4,128,384]{2,1,0:T(8,128)(2,1)S(1)}, u32[]{:S(2)}, u32[]{:S(2)}) collective-permute-start(bf16[4,128,384]{2,1,0:T(8,128)(2,1)S(1)} %bitcast_dynamic-update-slice_fusion.26), channel_id=1, source_target_pairs={{0,224},{1,225},{2,226},{3,227},{4,228},{5,229},{6,230},{7,231},{8... | collective-permute-start | bytes 1179656 | tf_op jit(solution)/shard_map/ppermute | solution.py:27
  94.6 7.0 %collective-permute-start.18 = (bf16[128,384]{1,0:T(8,128)(2,1)S(1)}, bf16[128,384]{1,0:T(8,128)(2,1)S(1)}, u32[]{:S(2)}, u32[]{:S(2)}) collective-permute-start(bf16[128,384]{1,0:T(8,128)(2,1)S(1)} %collective-permute-done.16), channel_id=1, source_target_pairs={{0,32},{1,33},{2,34},{3,35},{4,36},{5,37},{6,38},{7,39},{8,40},{9,... | collective-permute-start | bytes 294920 | tf_op jit(solution)/shard_map/ppermute | solution.py:27
  101.6 7.0 %collective-permute-start.19 = (bf16[128,384]{1,0:T(8,128)(2,1)S(1)}, bf16[128,384]{1,0:T(8,128)(2,1)S(1)}, u32[]{:S(2)}, u32[]{:S(2)}) collective-permute-start(bf16[128,384]{1,0:T(8,128)(2,1)S(1)} %collective-permute-done.17), channel_id=1, source_target_pairs={{0,224},{1,225},{2,226},{3,227},{4,228},{5,229},{6,230},{7,231},{8... | collective-permute-start | bytes 294920 | tf_op jit(solution)/shard_map/ppermute | solution.py:27
  108.6 6.1 %collective-permute-start.20 = (bf16[64,384]{1,0:T(8,128)(2,1)S(1)}, bf16[64,384]{1,0:T(8,128)(2,1)S(1)}, u32[]{:S(2)}, u32[]{:S(2)}) collective-permute-start(bf16[64,384]{1,0:T(8,128)(2,1)S(1)} %slice.116), channel_id=1, source_target_pairs={{0,32},{1,33},{2,34},{3,35},{4,36},{5,37},{6,38},{7,39},{8,40},{9,... | collective-permute-start | bytes 147464 | tf_op jit(solution)/shard_map/ppermute | solution.py:27
  114.7 4.3 %collective-permute-start.21 = (bf16[64,384]{1,0:T(8,128)(2,1)S(1)}, bf16[64,384]{1,0:T(8,128)(2,1)S(1)}, u32[]{:S(2)}, u32[]{:S(2)}) collective-permute-start(bf16[64,384]{1,0:T(8,128)(2,1)S(1)} %slice.117), channel_id=1, source_target_pairs={{0,224},{1,225},{2,226},{3,227},{4,228},{5,229},{6,230},{7,231},{8... | collective-permute-start | bytes 147464 | tf_op jit(solution)/shard_map/ppermute | solution.py:27
  119.0 36.3 %collective-permute-start.22 = (bf16[8,128,384]{2,1,0:T(8,128)(2,1)S(1)}, bf16[8,128,384]{2,1,0:T(8,128)(2,1)S(1)}, u32[]{:S(2)}, u32[]{:S(2)}) collective-permute-start(bf16[8,128,384]{2,1,0:T(8,128)(2,1)S(1)} %bitcast_dynamic-update-slice_fusion.24), channel_id=1, source_target_pairs={{0,4},{1,5},{2,6},{3,7},{4,16},{5,17},{6,18},{7,19},{8,12},{9,13},... | collective-permute-start | bytes 2359304 | tf_op jit(solution)/shard_map/ppermute | solution.py:27
  119.1 31.9 %collective-permute-start.8 = (bf16[4,128,384]{2,1,0:T(8,128)(2,1)S(1)}, bf16[4,128,384]{2,1,0:T(8,128)(2,1)S(1)}, u32[]{:S(2)}, u32[]{:S(2)}) collective-permute-start(bf16[4,128,384]{2,1,0:T(8,128)(2,1)S(1)} %collective-permute-done.6), channel_id=1, source_target_pairs={{0,32},{1,33},{2,34},{3,35},{4,36},{5,37},{6,38},{7,39},{8,40},{9,... | collective-permute-start | bytes 1179656 | tf_op jit(solution)/shard_map/ppermute | solution.py:27
  119.8 31.2 %collective-permute-start.9 = (bf16[4,128,384]{2,1,0:T(8,128)(2,1)S(1)}, bf16[4,128,384]{2,1,0:T(8,128)(2,1)S(1)}, u32[]{:S(2)}, u32[]{:S(2)}) collective-permute-start(bf16[4,128,384]{2,1,0:T(8,128)(2,1)S(1)} %collective-permute-done.7), channel_id=1, source_target_pairs={{0,224},{1,225},{2,226},{3,227},{4,228},{5,229},{6,230},{7,231},{8... | collective-permute-start | bytes 1179656 | tf_op jit(solution)/shard_map/ppermute | solution.py:27
  122.9 11.0 %collective-permute-start.38 = (bf16[4,1,256,128]{2,3,1,0:T(8,128)(2,1)S(1)}, bf16[4,1,256,128]{2,3,1,0:T(8,128)(2,1)S(1)}, u32[]{:S(2)}, u32[]{:S(2)}) collective-permute-start(bf16[4,1,256,128]{2,3,1,0:T(8,128)(2,1)S(1)} %slice.125), channel_id=1, source_target_pairs={{0,4},{1,5},{2,6},{3,7},{4,16},{5,17},{6,18},{7,19},{8,12},{9,13},... | collective-permute-start | bytes 786440 | tf_op jit(solution)/shard_map/ppermute | solution.py:27
  123.8 11.7 %collective-permute-start.39 = (bf16[4,1,256,128]{2,3,1,0:T(8,128)(2,1)S(1)}, bf16[4,1,256,128]{2,3,1,0:T(8,128)(2,1)S(1)}, u32[]{:S(2)}, u32[]{:S(2)}) collective-permute-start(bf16[4,1,256,128]{2,3,1,0:T(8,128)(2,1)S(1)} %slice.126), channel_id=1, source_target_pairs={{0,20},{1,21},{2,22},{3,23},{4,0},{5,1},{6,2},{7,3},{8,28},{9,29},... | collective-permute-start | bytes 786440 | tf_op jit(solution)/shard_map/ppermute | solution.py:27
  133.9 23.3 %collective-permute-start.23 = (bf16[8,128,384]{2,1,0:T(8,128)(2,1)S(1)}, bf16[8,128,384]{2,1,0:T(8,128)(2,1)S(1)}, u32[]{:S(2)}, u32[]{:S(2)}) collective-permute-start(bf16[8,128,384]{2,1,0:T(8,128)(2,1)S(1)} %bitcast_dynamic-update-slice_fusion.24), channel_id=1, source_target_pairs={{0,20},{1,21},{2,22},{3,23},{4,0},{5,1},{6,2},{7,3},{8,28},{9,29},... | collective-permute-start | bytes 2359304 | tf_op jit(solution)/shard_map/ppermute | solution.py:27
  136.2 64.4 %collective-permute-start.40 = (bf16[256,4096]{0,1:T(8,128)(2,1)}, bf16[256,4096]{0,1:T(8,128)(2,1)}, u32[]{:S(2)}, u32[]{:S(2)}) collective-permute-start(bf16[256,4096]{0,1:T(8,128)(2,1)} %bitcast.51), channel_id=1, source_target_pairs={{0,8},{1,9},{2,10},{3,11},{4,12},{5,13},{6,14},{7,15},{8,0},{9,1},... | collective-permute-start | bytes 6291464 | tf_op jit(solution)/shard_map/ppermute | solution.py:27
  151.0 12.0 %collective-permute-start.10 = (bf16[4,128,384]{2,1,0:T(8,128)(2,1)S(1)}, bf16[4,128,384]{2,1,0:T(8,128)(2,1)S(1)}, u32[]{:S(2)}, u32[]{:S(2)}) collective-permute-start(bf16[4,128,384]{2,1,0:T(8,128)(2,1)S(1)} %collective-permute-done.8), channel_id=1, source_target_pairs={{0,32},{1,33},{2,34},{3,35},{4,36},{5,37},{6,38},{7,39},{8,40},{9,... | collective-permute-start | bytes 1179656 | tf_op jit(solution)/shard_map/ppermute | solution.py:27
  151.0 12.1 %collective-permute-start.11 = (bf16[4,128,384]{2,1,0:T(8,128)(2,1)S(1)}, bf16[4,128,384]{2,1,0:T(8,128)(2,1)S(1)}, u32[]{:S(2)}, u32[]{:S(2)}) collective-permute-start(bf16[4,128,384]{2,1,0:T(8,128)(2,1)S(1)} %collective-permute-done.9), channel_id=1, source_target_pairs={{0,224},{1,225},{2,226},{3,227},{4,228},{5,229},{6,230},{7,231},{8... | collective-permute-start | bytes 1179656 | tf_op jit(solution)/shard_map/ppermute | solution.py:27
  155.3 19.1 %collective-permute-start.24 = (bf16[4,128,384]{2,1,0:T(8,128)(2,1)S(1)}, bf16[4,128,384]{2,1,0:T(8,128)(2,1)S(1)}, u32[]{:S(2)}, u32[]{:S(2)}) collective-permute-start(bf16[4,128,384]{2,1,0:T(8,128)(2,1)S(1)} %slice.118), channel_id=1, source_target_pairs={{0,4},{1,5},{2,6},{3,7},{4,16},{5,17},{6,18},{7,19},{8,12},{9,13},... | collective-permute-start | bytes 1179656 | tf_op jit(solution)/shard_map/ppermute | solution.py:27
  157.2 18.1 %collective-permute-start.25 = (bf16[4,128,384]{2,1,0:T(8,128)(2,1)S(1)}, bf16[4,128,384]{2,1,0:T(8,128)(2,1)S(1)}, u32[]{:S(2)}, u32[]{:S(2)}) collective-permute-start(bf16[4,128,384]{2,1,0:T(8,128)(2,1)S(1)} %slice.119), channel_id=1, source_target_pairs={{0,20},{1,21},{2,22},{3,23},{4,0},{5,1},{6,2},{7,3},{8,28},{9,29},... | collective-permute-start | bytes 1179656 | tf_op jit(solution)/shard_map/ppermute | solution.py:27
  163.0 6.9 %collective-permute-start.12 = (bf16[2,128,384]{2,1,0:T(8,128)(2,1)S(1)}, bf16[2,128,384]{2,1,0:T(8,128)(2,1)S(1)}, u32[]{:S(2)}, u32[]{:S(2)}) collective-permute-start(bf16[2,128,384]{2,1,0:T(8,128)(2,1)S(1)} %slice.113), channel_id=1, source_target_pairs={{0,32},{1,33},{2,34},{3,35},{4,36},{5,37},{6,38},{7,39},{8,40},{9,... | collective-permute-start | bytes 589832 | tf_op jit(solution)/shard_map/ppermute | solution.py:27
  163.1 7.5 %collective-permute-start.13 = (bf16[2,128,384]{2,1,0:T(8,128)(2,1)S(1)}, bf16[2,128,384]{2,1,0:T(8,128)(2,1)S(1)}, u32[]{:S(2)}, u32[]{:S(2)}) collective-permute-start(bf16[2,128,384]{2,1,0:T(8,128)(2,1)S(1)} %slice.114), channel_id=1, source_target_pairs={{0,224},{1,225},{2,226},{3,227},{4,228},{5,229},{6,230},{7,231},{8... | collective-permute-start | bytes 589832 | tf_op jit(solution)/shard_map/ppermute | solution.py:27
  187.1 5.0 %copy-start.12 = (bf16[1024,768]{0,1:T(8,128)(2,1)}, bf16[1024,768]{0,1:T(8,128)(2,1)S(1)}, u32[]{:S(2)}) copy-start(bf16[1024,768]{0,1:T(8,128)(2,1)S(1)} %convolution_convert_fusion.2) | copy-start | bytes 4718596
  198.4 2.9 collective-permute-start.26
  201.3 3.8 %copy-start.7 = (bf16[512,256]{1,0:T(8,128)(2,1)}, bf16[512,256]{1,0:T(8,128)(2,1)S(1)}, u32[]{:S(2)}) copy-start(bf16[512,256]{1,0:T(8,128)(2,1)S(1)} %collective-permute-done.26) | copy-start | bytes 786436
  205.2 14.4 %collective-permute-start.41 = (bf16[64,4096]{1,0:T(8,128)(2,1)S(1)}, bf16[64,4096]{1,0:T(8,128)(2,1)S(1)}, u32[]{:S(2)}, u32[]{:S(2)}) collective-permute-start(bf16[64,4096]{1,0:T(8,128)(2,1)S(1)} %get-tuple-element.4), channel_id=1, source_target_pairs={{0,1},{1,2},{2,3},{3,0},{4,5},{5,6},{6,7},{7,4},{8,9},{9,10},{10,1... | collective-permute-start | bytes 1572872 | tf_op jit(solution)/shard_map/ppermute | solution.py:27
  206.7 5.3 %copy-start.8 = (bf16[512,256]{1,0:T(8,128)(2,1)S(1)}, bf16[512,256]{1,0:T(8,128)(2,1)}, u32[]{:S(2)}) copy-start(bf16[512,256]{1,0:T(8,128)(2,1)} %copy-done.7) | copy-start | bytes 786436
  210.6 13.1 %collective-permute-start.43 = (bf16[64,4096]{1,0:T(8,128)(2,1)S(1)}, bf16[64,4096]{1,0:T(8,128)(2,1)S(1)}, u32[]{:S(2)}, u32[]{:S(2)}) collective-permute-start(bf16[64,4096]{1,0:T(8,128)(2,1)S(1)} %get-tuple-element.5), channel_id=1, source_target_pairs={{0,3},{1,0},{2,1},{3,2},{4,7},{5,4},{6,5},{7,6},{8,11},{9,8},{10,9... | collective-permute-start | bytes 1572872 | tf_op jit(solution)/shard_map/ppermute | solution.py:27
  219.8 24.8 %collective-permute-start.42 = (bf16[128,4096]{1,0:T(8,128)(2,1)S(1)}, bf16[128,4096]{1,0:T(8,128)(2,1)}, u32[]{:S(2)}, u32[]{:S(2)}) collective-permute-start(bf16[128,4096]{1,0:T(8,128)(2,1)S(1)} %pad_maximum_fusion.1), channel_id=1, source_target_pairs={{0,1},{1,2},{2,3},{3,0},{4,5},{5,6},{6,7},{7,4},{8,9},{9,10},{10,1... | collective-permute-start | bytes 3145736 | tf_op jit(solution)/shard_map/ppermute | solution.py:27
  224.8 23.7 %collective-permute-start.44 = (bf16[128,4096]{1,0:T(8,128)(2,1)}, bf16[128,4096]{1,0:T(8,128)(2,1)}, u32[]{:S(2)}, u32[]{:S(2)}) collective-permute-start(bf16[128,4096]{1,0:T(8,128)(2,1)} %pad_maximum_fusion.2), channel_id=1, source_target_pairs={{0,3},{1,0},{2,1},{3,2},{4,7},{5,4},{6,5},{7,6},{8,11},{9,8},{10,9... | collective-permute-start | bytes 3145736 | tf_op jit(solution)/shard_map/ppermute | solution.py:27
  227.2 21.2 %copy-start.9 = (bf16[512,256]{1,0:T(8,128)(2,1)S(1)}, bf16[512,256]{1,0:T(8,128)(2,1)}, u32[]{:S(2)}) copy-start(bf16[512,256]{1,0:T(8,128)(2,1)} %copy-done.7) | copy-start | bytes 786436
  253.6 24.0 %copy-start.2 = (bf16[128,512]{1,0:T(8,128)(2,1)}, bf16[128,512]{1,0:T(8,128)(2,1)S(1)}, u32[]{:S(2)}) copy-start(bf16[128,512]{1,0:T(8,128)(2,1)S(1)} %convolution_convert_fusion.4) | copy-start | bytes 393220
  253.6 9.2 %collective-permute-start.47 = (bf16[128,512]{1,0:T(8,128)(2,1)S(1)}, bf16[128,512]{1,0:T(8,128)(2,1)S(1)}, u32[]{:S(2)}, u32[]{:S(2)}) collective-permute-start(bf16[128,512]{1,0:T(8,128)(2,1)S(1)} %convolution_convert_fusion.4), channel_id=1, source_target_pairs={{0,128},{1,129},{2,130},{3,131},{4,132},{5,133},{6,134},{7,135},{8... | collective-permute-start | bytes 393224 | tf_op jit(solution)/shard_map/ppermute | solution.py:27
  262.8 11.8 %collective-permute-start.48 = (bf16[128,512]{1,0:T(8,128)(2,1)S(1)}, bf16[128,512]{1,0:T(8,128)(2,1)S(1)}, u32[]{:S(2)}, u32[]{:S(2)}) collective-permute-start(bf16[128,512]{1,0:T(8,128)(2,1)S(1)} %collective-permute-done.47), channel_id=1, source_target_pairs={{0,1},{1,2},{2,3},{3,0},{4,5},{5,6},{6,7},{7,4},{8,9},{9,10},{10,1... | collective-permute-start | bytes 393224 | tf_op jit(solution)/shard_map/ppermute | solution.py:27
  263.8 10.9 %collective-permute-start.49 = (bf16[128,512]{1,0:T(8,128)(2,1)S(1)}, bf16[128,512]{1,0:T(8,128)(2,1)S(1)}, u32[]{:S(2)}, u32[]{:S(2)}) collective-permute-start(bf16[128,512]{1,0:T(8,128)(2,1)S(1)} %collective-permute-done.47), channel_id=1, source_target_pairs={{0,2},{1,3},{2,0},{3,1},{4,6},{5,7},{6,4},{7,5},{8,10},{9,11},{10,... | collective-permute-start | bytes 393224 | tf_op jit(solution)/shard_map/ppermute | solution.py:27
  267.4 7.3 %collective-permute-start.50 = (bf16[128,512]{1,0:T(8,128)(2,1)S(1)}, bf16[128,512]{1,0:T(8,128)(2,1)S(1)}, u32[]{:S(2)}, u32[]{:S(2)}) collective-permute-start(bf16[128,512]{1,0:T(8,128)(2,1)S(1)} %collective-permute-done.47), channel_id=1, source_target_pairs={{0,3},{1,0},{2,1},{3,2},{4,7},{5,4},{6,5},{7,6},{8,11},{9,8},{10,9... | collective-permute-start | bytes 393224 | tf_op jit(solution)/shard_map/ppermute | solution.py:27
  267.4 33.5 %collective-permute-start.45 = (bf16[128,4096]{1,0:T(8,128)(2,1)S(1)}, bf16[128,4096]{1,0:T(8,128)(2,1)S(1)}, u32[]{:S(2)}, u32[]{:S(2)}) collective-permute-start(bf16[128,4096]{1,0:T(8,128)(2,1)S(1)} %fusion.7), channel_id=1, source_target_pairs={{0,0},{1,1},{2,2},{3,3},{4,8},{5,9},{6,10},{7,11},{8,4},{9,5},{10,... | collective-permute-start | bytes 3145736 | tf_op jit(solution)/shard_map/ppermute | solution.py:27
  276.2 6.0 %collective-permute-start.51 = (bf16[512,512]{1,0:T(8,128)(2,1)}, bf16[512,512]{1,0:T(8,128)(2,1)S(1)}, u32[]{:S(2)}, u32[]{:S(2)}) collective-permute-start(bf16[512,512]{1,0:T(8,128)(2,1)} %pad_maximum_fusion.3), channel_id=1, source_target_pairs={{0,8},{1,9},{2,10},{3,11},{4,12},{5,13},{6,14},{7,15},{8,0},{9,1},... | collective-permute-start | bytes 1572872 | tf_op jit(solution)/shard_map/ppermute | solution.py:27
  294.7 6.3 %collective-permute-start.52 = (bf16[128,512]{1,0:T(8,128)(2,1)S(1)}, bf16[128,512]{1,0:T(8,128)(2,1)S(1)}, u32[]{:S(2)}, u32[]{:S(2)}) collective-permute-start(bf16[128,512]{1,0:T(8,128)(2,1)S(1)} %fusion.23), channel_id=1, source_target_pairs={{0,0},{1,1},{2,2},{3,3},{4,8},{5,9},{6,10},{7,11},{8,4},{9,5},{10,... | collective-permute-start | bytes 393224 | tf_op jit(solution)/shard_map/ppermute | solution.py:27
  (4 other events, 6.3 us)
Sparse Core Ops, SparseCore 0:
  27.6 55.3 all-gather.2
  84.8 48.1 all-gather.4
